TPU v7x, 256 devices: a whole 4x4x8 slice. The times are simulated.
256 devices in a mesh: cmp: 32 (over y, z_hi, core), asy: 8 (over x, z_lo).
Axes of the slice: x: 4, y: 4, z: 8 (z_hi: 4, z_lo: 2; z = z_hi * 2 + z_lo), core: 2. Of those that a mesh axis runs over, the one named last changes fastest.
Arguments:
- comp_emb: bfloat16 [65536, 256], P(('cmp', 'asy')), may hold values from -6 to 6
- assay_emb: bfloat16 [32768, 256], P(('asy', 'cmp')), may hold values from -6 to 6
- bilinear: bfloat16 [256, 256], replicated, may hold values from -3 to 3
- tile_pos: int32 [128, 64], P('cmp', 'asy'), may hold values 0 or 1
Outputs:
- grad_comp: float32 [65536, 256], P(('cmp', 'asy'))
- grad_assay: float32 [32768, 256], P(('asy', 'cmp'))
- grad_bilinear: float32 [256, 256], replicated
All inputs are finite; a program needn't handle non-finite values. No bound on the sum of `tile_pos` on one device may be relied on, other than what follows from the above.
Results may differ from a plain program's by a relative error of at most 0.0004.
The roundings to bfloat16 on the way count: a program that leaves them out, or rounds other values in their place, can miss the bound.
Values may be sent and summed in bfloat16 or wider, within the bound.
A program may use at most 128 MiB of HBM per device.

v0:
```python
import math

import jax
import jax.numpy as jnp
from jax import lax
from jax.sharding import PartitionSpec as P


def row_onehot(count, tile_rows, tiles):
    index = jnp.arange(count, dtype=jnp.int32) // tile_rows
    return (index[:, None] == jnp.arange(tiles, dtype=jnp.int32)[None, :]).astype(jnp.float32)


def col_onehot(count, tile_rows, tiles):
    index = jnp.arange(count, dtype=jnp.int32) // tile_rows
    return (jnp.arange(tiles, dtype=jnp.int32)[:, None] == index[None, :]).astype(jnp.float32)


def local(comp_emb, assay_emb, bilinear, tile_pos):
    size_cmp = lax.axis_size("cmp")
    size_asy = lax.axis_size("asy")
    width = comp_emb.shape[1]
    comp_block = lax.all_gather(comp_emb, "asy", axis=0, tiled=True)
    query = jnp.dot(comp_block, bilinear, preferred_element_type=jnp.float32).astype(jnp.bfloat16)
    block_rows = comp_block.shape[0]
    assay_rows = assay_emb.shape[0] * size_cmp
    total_comp = comp_emb.shape[0] * size_asy * size_cmp
    total_assay = assay_rows * size_asy
    row_tiles = tile_pos.shape[0]
    col_tiles = tile_pos.shape[1]
    tile_rows = block_rows // row_tiles
    scale = 1.0 / math.sqrt(width)
    weight_f32 = bilinear.astype(jnp.float32)
    row_labels = jnp.dot(row_onehot(block_rows, tile_rows, row_tiles), tile_pos.astype(jnp.float32))
    piece = lax.all_gather(assay_emb, "cmp", axis=0, tiled=True)
    count = piece.shape[0]
    scores = (
        lax.dot_general(query, piece, (((1,), (1,)), ((), ())), preferred_element_type=jnp.float32)
        * scale
    )
    labels = jnp.dot(row_labels, col_onehot(count, tile_rows, col_tiles))
    slope = (jax.nn.sigmoid(scores) - labels).astype(jnp.bfloat16)
    sums = jnp.dot(slope, piece, preferred_element_type=jnp.float32)
    part = lax.dot_general(
        slope, query, (((0,), (0,)), ((), ())), preferred_element_type=jnp.float32
    )
    grads = part
    sums, grads = (sums, grads)
    own_assay = assay_emb.shape[0]
    whole = lax.psum(grads, "cmp")
    mine = lax.dynamic_slice_in_dim(whole, lax.axis_index("cmp") * own_assay, own_assay, 0)
    grad_assay = mine / math.sqrt(total_comp)
    comp_part = lax.dot_general(
        sums, weight_f32, (((1,), (1,)), ((), ())), precision=lax.Precision.HIGHEST
    )
    grad_comp = lax.psum_scatter(comp_part, "asy", scatter_dimension=0, tiled=True) / math.sqrt(
        total_assay
    )
    weight_part = lax.dot_general(
        comp_block.astype(jnp.float32),
        sums,
        (((0,), (0,)), ((), ())),
        precision=lax.Precision.HIGHEST,
    )
    grad_bilinear = lax.psum(weight_part, ("cmp", "asy")) / math.sqrt(total_comp * total_assay)
    return (grad_comp, grad_assay, grad_bilinear)


def solution(mesh):
    return jax.shard_map(
        local,
        mesh=mesh,
        in_specs=(P(("cmp", "asy"), None), P(("asy", "cmp"), None), P(), P("cmp", "asy")),
        out_specs=(P(("cmp", "asy"), None), P(("asy", "cmp"), None), P()),
        check_vma=False,
    )
```

profile of v0, /device:TPU:32, one launch (start us, length us, event | category | flops | bytes accessed | tf_op | source)
XLA Modules:
  0.0 756.6 jit_solution(11756872526193142396)
XLA Ops:
  7.2 0.0 copy-start
  7.2 0.0 all-gather.3.cloned.1.call-start
  7.2 0.7 all-gather.3.cloned.1.call-update
  7.9 0.0 all-gather.5.cloned.1.call-start
  8.0 0.7 all-gather.5.cloned.1.call-update
  8.7 0.0 all-reduce.5.cloned.1.call-start
  8.7 14.1 %fusion = f32[2048,4096]{1,0:T(8,128)} fusion(s32[2048]{0:T(1024)S(1)} %add_select_fusion.1, s32[4096]{0:T(1024)S(1)} %add_select_fusion, s32[4,8]{1,0:T(4,128)} %param.7), kind=kOutput, calls=%fused_computation.2 | convolution fusion | flops 134389792 | bytes 33579136 | tf_op jit(solution)/shard_map/dot_general | solution.py:41
  22.9 30.4 %all-gather.3.cloned.1.call-done = bf16[2048,256]{1,0:T(8,128)(2,1)} async-done(((bf16[256,256]{1,0:T(8,128)(2,1)}), bf16[2048,256]{1,0:T(8,128)(2,1)}) %all-gather.3.cloned.1.call-update) | async-done | bytes 1048592 | tf_op jit(solution)/shard_map/all_gather | solution.py:23
  53.2 0.0 copy-done
  53.2 1.7 convolution_convert_fusion
  54.9 55.0 %all-gather.5.cloned.1.call-done = bf16[4096,256]{1,0:T(8,128)(2,1)} async-done(((bf16[128,256]{1,0:T(8,128)(2,1)}), bf16[4096,256]{1,0:T(8,128)(2,1)}) %all-gather.5.cloned.1.call-update) | async-done | bytes 2097168 | tf_op jit(solution)/shard_map/all_gather | solution.py:35
  109.9 20.1 %subtract_convert_fusion = bf16[2048,4096]{1,0:T(8,128)(2,1)} fusion(f32[2048,4096]{1,0:T(8,128)} %fusion, bf16[2048,256]{1,0:T(8,128)(2,1)S(1)} %convolution_convert_fusion, bf16[4096,256]{1,0:T(8,128)(2,1)} %all-gather.5.cloned.1.call-done), kind=kOutput, calls=%fused_computation | convolution fusion | flops 4345298944 | bytes 53477376 | tf_op jit(solution)/shard_map/dot_general | solution.py:38
  130.0 0.0 copy-start.1
  130.0 8.8 %fusion.14 = f32[2048,256]{1,0:T(8,128)S(1)} fusion(bf16[2048,4096]{1,0:T(8,128)(2,1)} %subtract_convert_fusion, bf16[4096,256]{1,0:T(8,128)(2,1)} %all-gather.5.cloned.1.call-done), kind=kOutput, calls=%fused_computation.27 | convolution fusion | flops 4294967296 | bytes 20971520 | tf_op jit(solution)/shard_map/dot_general | solution.py:43
  138.8 0.0 copy-done.1
  138.8 2.5 convolution_bitcast_fusion
  141.4 0.0 all-reduce.5.cloned.1.call-update
  141.4 0.0 reduce-scatter.2.cloned.1.call-start
  141.4 2.4 fusion.15
  143.9 0.0 reduce-scatter.2.cloned.1.call-update
  143.9 0.2 all-reduce.3.cloned.1.call-start
  144.1 10.2 %fusion.16 = f32[4096,256]{1,0:T(8,128)} fusion(bf16[2048,4096]{1,0:T(8,128)(2,1)} %subtract_convert_fusion, bf16[2048,256]{1,0:T(8,128)(2,1)S(1)} %convolution_convert_fusion), kind=kOutput, calls=%fused_computation.29 | convolution fusion | flops 4294967296 | bytes 22020096 | tf_op jit(solution)/shard_map/dot_general | solution.py:44
  154.4 0.0 all-reduce.3.cloned.1.call-update
  154.4 234.1 %all-reduce.5.cloned.1.call-done = f32[256,256]{0,1:T(8,128)} async-done(((f32[256,256]{0,1:T(8,128)}), f32[256,256]{0,1:T(8,128)}) %all-reduce.5.cloned.1.call-update) | async-done | bytes 262160 | tf_op jit(solution)/shard_map/psum | solution.py:65
  388.5 1.0 broadcast_multiply_fusion
  389.5 0.8 copy.7
  390.3 54.7 %reduce-scatter.2.cloned.1.call-done = f32[256,256]{1,0:T(8,128)} async-done(((f32[2048,256]{1,0:T(8,128)}), f32[256,256]{1,0:T(8,128)}) %reduce-scatter.2.cloned.1.call-update) | async-done | bytes 262160 | tf_op jit(solution)/shard_map/reduce_scatter | solution.py:56
  445.0 1.7 broadcast_multiply_fusion.1
  446.7 301.8 %all-reduce.3.cloned.1.call-done = f32[4096,256]{1,0:T(8,128)} async-done(((f32[4096,256]{1,0:T(8,128)}), f32[4096,256]{1,0:T(8,128)}) %all-reduce.3.cloned.1.call-update) | async-done | bytes 4194320 | tf_op jit(solution)/shard_map/psum | solution.py:50
  748.5 1.6 dynamic-slice_multiply_fusion
  (2 shorter events, 0.0 us)
Async XLA Ops:
  7.2 46.1 %copy-start = (bf16[256,256]{1,0:T(8,128)(2,1)S(1)}, bf16[256,256]{1,0:T(8,128)(2,1)}, u32[]{:S(2)}) copy-start(bf16[256,256]{1,0:T(8,128)(2,1)} %param.6) | copy-start | bytes 393220
  7.2 46.1 %all-gather.3.cloned.1.call-start = ((), (), s32[]{:S(2)}) async-start(), calls=%async_computation.1 | async-start | bytes 1179648 | tf_op jit(solution)/shard_map/all_gather | solution.py:23
  7.9 102.0 %all-gather.5.cloned.1.call-start = ((), (), s32[]{:S(2)}) async-start(), calls=%async_computation.2 | async-start | bytes 2162688 | tf_op jit(solution)/shard_map/all_gather | solution.py:35
  8.7 379.8 %all-reduce.5.cloned.1.call-start = ((), (), s32[]{:S(2)}) async-start(), calls=%async_computation.5 | async-start | bytes 524288 | tf_op jit(solution)/shard_map/psum | solution.py:65
  130.0 8.8 %copy-start.1 = (bf16[2048,256]{1,0:T(8,128)(2,1)S(1)}, bf16[2048,256]{1,0:T(8,128)(2,1)}, u32[]{:S(2)}) copy-start(bf16[2048,256]{1,0:T(8,128)(2,1)} %all-gather.3.cloned.1.call-done) | copy-start | bytes 3145732
  141.4 303.6 %reduce-scatter.2.cloned.1.call-start = ((), (), s32[]{:S(2)}) async-start(), calls=%async_computation.3 | async-start | bytes 2359296 | tf_op jit(solution)/shard_map/reduce_scatter | solution.py:56
  143.9 604.6 %all-reduce.3.cloned.1.call-start = ((), (), s32[]{:S(2)}) async-start(), calls=%async_computation.4 | async-start | bytes 8388608 | tf_op jit(solution)/shard_map/psum | solution.py:50
Sparse Core Ops, SparseCore 0:
  9.8 43.3 all-gather.2
  55.8 54.0 all-gather.4
  141.5 246.9 all-reduce.4
  390.9 54.0 reduce-scatter.1
  447.5 300.9 all-reduce.2
where the time goes:
time: 757 us
  waiting for transfers between devices  677 us (89%)
  matrix products  59.9 us (8%)
  between operations  13.8 us (2%)
    psum x1, waiting for transfers between devices, local(): whole = lax.psum(grads, 'cmp')  302 us
    psum x1, waiting for transfers between devices, local(): lax.psum(weight_part, ('cmp', 'asy')) / math.sqrt(total_comp * total_assay)  234 us
    all_gather x1, waiting for transfers between devices, local(): piece = lax.all_gather(assay_emb, 'cmp', axis=0, tiled=True)  55 us
    reduce_scatter x1, waiting for transfers between devices, local(): lax.psum_scatter(comp_part, 'asy', scatter_dimension=0, tiled=True)  54.7 us
    all_gather x1, waiting for transfers between devices, local(): comp_block = lax.all_gather(comp_emb, 'asy', axis=0, tiled=True)  30.4 us
    dot_general x1, matrix products, local(): lax.dot_general(query, piece, (((1,), (1,)), ((), ())), preferred_element...  20.1 us
  transfers between devices with their start and end apart: 5, of which 5 were waited for; matrix products, arithmetic and copies ran while one was open for 4% of the time, Pallas kernels for 0%

commit v1 on v0

v1 whole, which is shorter than its diff:
```python
import functools
import math

import jax
import jax.numpy as jnp
from jax import lax
from jax.experimental import pallas as pl
from jax.experimental.pallas import tpu as pltpu
from jax.sharding import PartitionSpec as P

MESH = pl.DeviceIdType.MESH
NN = (((1,), (0,)), ((), ()))
NT = (((1,), (1,)), ((), ()))
TN = (((0,), (0,)), ((), ()))
LEVELS = 32000.0
CODE_ROWS = 16
RING = 4


def dot(lhs, rhs, dims):
    return lax.dot_general(lhs, rhs, dims, preferred_element_type=jnp.float32)


def split_bf16(value):
    high = value.astype(jnp.bfloat16)
    low = (value - high.astype(jnp.float32)).astype(jnp.bfloat16)
    return high, low


def encode(value, target, row):
    rows = value.shape[0]
    top = jnp.maximum(jnp.max(jnp.abs(value), axis=0, keepdims=True), 1e-30)
    code = jnp.ceil(jnp.log2(top) * 256.0) + 1.0
    scale = LEVELS * jnp.exp2(code * (-1.0 / 256.0))
    target[pl.ds(row, rows), :] = jnp.round(value * scale).astype(jnp.int32).astype(jnp.int16)
    target[pl.ds(row + rows, CODE_ROWS), :] = (
        jnp.broadcast_to(code, (CODE_ROWS, value.shape[1])).astype(jnp.int32).astype(jnp.int16)
    )


def decode(source, row, rows):
    code = source[pl.ds(row + rows, CODE_ROWS), :].astype(jnp.int32).astype(jnp.float32)[0:1, :]
    unit = jnp.exp2(code * (1.0 / 256.0)) * (1.0 / LEVELS)
    return source[pl.ds(row, rows), :].astype(jnp.int32).astype(jnp.float32) * unit


class Sends:
    def __init__(self, send_sems, recv_sems):
        self.send_sems, self.recv_sems = send_sems, recv_sems
        self.count = 0
        self.started = []

    def make(self, source, target, device):
        index = self.count
        self.count += 1
        return pltpu.make_async_remote_copy(
            src_ref=source,
            dst_ref=target,
            send_sem=self.send_sems.at[index],
            recv_sem=self.recv_sems.at[index],
            device_id=device,
            device_id_type=MESH,
        )

    def start(self, source, target, device):
        copy = self.make(source, target, device)
        copy.start()
        self.started.append(copy)
        return copy

    def finish(self):
        for copy in self.started:
            copy.wait_send()


SENDS = 80


def kernel(
    totals,
    tile_pos,
    comp_ref,
    assay_ref,
    bil_ref,
    gc_ref,
    ga_ref,
    gb_ref,
    comps,
    assays,
    query,
    slope,
    pulled,
    grads,
    grads_in,
    pull_out,
    pull_in,
    pull_z_out,
    pull_z_in,
    grad_out,
    grad_in,
    grad_z_out,
    grad_z_in,
    weight,
    weight_x,
    weight_y,
    weight_z,
    weight_l,
    weight_c,
    weight_g,
    send_sems,
    recv_sems,
    local_sems,
):
    total_comp, total_assay, width = totals
    cmp, asy = lax.axis_index("cmp"), lax.axis_index("asy")
    c, zh, y = cmp % 2, (cmp // 2) % RING, cmp // (2 * RING)
    zl, x = asy % 2, asy // 2
    oc = 1 - c

    def at(y_=None, zh_=None, c_=None, x_=None, zl_=None):
        y_ = y if y_ is None else y_
        zh_ = zh if zh_ is None else zh_
        c_ = c if c_ is None else c_
        x_ = x if x_ is None else x_
        zl_ = zl if zl_ is None else zl_
        return ((y_ * RING + zh_) * 2 + c_, x_ * 2 + zl_)

    def turn(place, step):
        return lax.rem(place + step, RING)

    AWAY = (1, 3, 2)
    peer_c = at(c_=oc)
    peer_l = at(zl_=1 - zl)
    peer_x = {d: at(x_=turn(x, d)) for d in AWAY}
    peer_y = {d: at(y_=turn(y, d)) for d in AWAY}
    peer_z = {d: at(zh_=turn(zh, d)) for d in AWAY}
    partners = [peer_c, peer_l, *peer_x.values(), *peer_y.values(), *peer_z.values()]

    barrier = pltpu.get_barrier_semaphore()
    for partner in partners:
        pl.semaphore_signal(barrier, inc=1, device_id=partner, device_id_type=MESH)

    rows_c, rows_a = comp_ref.shape[0], assay_ref.shape[0]
    own_comp = pltpu.make_async_copy(comp_ref, comps.at[x, pl.ds(zl * rows_c, rows_c)], local_sems.at[0])
    own_assay = pltpu.make_async_copy(assay_ref, assays.at[c, y, pl.ds(zh * rows_a, rows_a)], local_sems.at[1])
    own_comp.start()
    own_assay.start()
    pl.semaphore_wait(barrier, len(partners))

    net = Sends(send_sems, recv_sems)

    def comp_rows(x_, zl_):
        return comps.at[x_, pl.ds(zl_ * rows_c, rows_c)]

    def assay_rows(y_, zh_):
        return assays.at[c, y_, pl.ds(zh_ * rows_a, rows_a)]

    c_l = net.start(comp_ref, comp_rows(x, zl), peer_l)
    a_z = {d: net.start(assay_ref, assay_rows(y, zh), peer_z[d]) for d in AWAY}
    c_x, c_f, a_y, a_f = {}, {}, {}, {}
    for d in AWAY:
        c_x[d] = net.start(comp_ref, comp_rows(x, zl), peer_x[d])
        a_y[d] = net.start(assay_ref, assay_rows(y, zh), peer_y[d])

    def make_query(k, row, rows):
        block = comps[k, pl.ds(row, rows), :]
        query[k, pl.ds(row, rows), :] = dot(block, bil_ref[...], NN).astype(jnp.bfloat16)

    pulled[...] = jnp.zeros_like(pulled)
    own_comp.wait()
    make_query(x, zl * rows_c, rows_c)
    c_l.wait_recv()
    for d in AWAY:
        block = comp_rows(x, 1 - zl)
        c_f[d] = net.start(block, block, peer_x[d])
    make_query(x, (1 - zl) * rows_c, rows_c)
    own_assay.wait()
    for d in AWAY:
        a_z[d].wait_recv()
        block = assay_rows(y, turn(zh, RING - d))
        for e in AWAY:
            a_f[d, e] = net.start(block, block, peer_y[e])

    a_c = {}

    def share(d):
        block = assays.at[c, turn(y, RING - d)]
        a_c[d] = net.start(block, block, peer_c)

    share(0)

    scale = 1.0 / math.sqrt(width)
    half = slope.shape[3] // 2

    def score(k, cc, l):
        chunk = assays[cc, l]
        q = query[k]
        scores = dot(q * jnp.bfloat16(scale), chunk, NT)
        sig = 1.0 / (1.0 + jnp.exp(-scores))
        for h in range(2):
            label = tile_pos[k, 2 * l + h].astype(jnp.float32)
            slope[k, cc * RING + l, :, h * half : (h + 1) * half] = (
                sig[:, h * half : (h + 1) * half] - label
            ).astype(jnp.bfloat16)
        pulled[k] = pulled[k] + dot(slope[k, cc * RING + l], chunk, NN)

    def score_near(cc, l):
        @pl.loop(0, 3)
        def _(i):
            score(turn(x, i + i // 2), cc, l)

    def arrive_assay(d):
        a_y[d].wait_recv()
        for e in AWAY:
            a_f[e, d].wait_recv()
        share(d)

    def arrive_comp(d):
        c_x[d].wait_recv()
        c_f[d].wait_recv()
        make_query(turn(x, RING - d), 0, 2 * rows_c)

    l1, l3, l2 = turn(y, 3), turn(y, 1), turn(y, 2)
    score(x, c, y)
    a_c[0].wait_recv()
    score(x, oc, y)
    arrive_comp(1)
    arrive_comp(3)
    arrive_assay(1)
    arrive_assay(3)

    @pl.loop(0, 2)
    def _(i):
        k = turn(x, 1 + 2 * i)
        score(k, c, y)
        score(k, oc, y)

    score_near(c, l1)
    score_near(c, l3)
    a_c[1].wait_recv()
    score_near(oc, l1)
    a_c[3].wait_recv()
    score_near(oc, l3)
    arrive_assay(2)
    arrive_comp(2)
    score_near(c, l2)
    a_c[2].wait_recv()
    score_near(oc, l2)

    def send_pulled(d):
        k = turn(x, d)
        slot = AWAY.index(d)
        for h in range(2):
            encode(pulled[k, h * rows_c : (h + 1) * rows_c, :], pull_out.at[slot], h * (rows_c + CODE_ROWS))
        return net.start(pull_out.at[slot], pull_in.at[slot], peer_x[d])

    p_x = {1: send_pulled(1), 3: send_pulled(3)}

    k2 = turn(x, 2)
    score(k2, c, l2)
    score(k2, oc, l2)

    def grad(cc, l):
        left = slope[:, cc * RING + l].reshape(RING * slope.shape[2], slope.shape[3])
        right = query[...].reshape(RING * query.shape[1], query.shape[2])
        grads[cc, l] = dot(left, right, TN)

    g_c, g_y = {}, {}

    def grad_both(d):
        l = turn(y, d)
        grad(oc, l)
        g_c[d] = net.start(grads.at[oc, l], grads_in.at[l], peer_c)
        grad(c, l)

    def send_grad(d):
        l = turn(y, d)
        g_c[d].wait_recv()
        slot = AWAY.index(d)
        for h in range(RING):
            rows = pl.ds(h * rows_a, rows_a)
            encode(grads[c, l, rows, :] + grads_in[l, rows, :], grad_out.at[slot], h * (rows_a + CODE_ROWS))
        g_y[d] = net.start(grad_out.at[slot], grad_in.at[slot], peer_y[d])

    grad_both(2)

    @pl.loop(0, 4)
    def _(i):
        l = turn(y, 1 + 2 * (i % 2))
        score(k2, (c + i // 2) % 2, l)

    score(k2, c, y)
    score(k2, oc, y)
    p_x[2] = send_pulled(2)
    send_grad(2)
    grad_both(1)
    grad_both(3)
    send_grad(1)

    def weight_term(k):
        high, low = split_bf16(pulled[k])
        return dot(comps[k], high, TN) + dot(comps[k], low, TN)

    weight[...] = jnp.zeros_like(weight)

    @pl.loop(0, RING)
    def _(k):
        weight[...] += weight_term(k)

    part_x, part_y = width // RING, width // RING // RING
    w_x = {}
    for d in AWAY:
        w_x[d] = net.start(
            weight.at[pl.ds(turn(x, d) * part_x, part_x)], weight_x.at[AWAY.index(d)], peer_x[d]
        )
    send_grad(3)
    grad_both(0)

    w_y = {}
    for d in AWAY:
        w_x[d].wait_recv()
    mine = weight.at[pl.ds(x * part_x, part_x)]
    mine[...] = mine[...] + weight_x[0] + weight_x[1] + weight_x[2]
    for d in AWAY:
        w_y[d] = net.start(
            weight.at[pl.ds(x * part_x + turn(y, d) * part_y, part_y)],
            weight_y.at[AWAY.index(d)],
            peer_y[d],
        )

    for d in AWAY:
        p_x[d].wait_recv()

    def pulled_rows(h):
        value = pulled[x, pl.ds(h * rows_c, rows_c), :]
        for slot in range(3):
            value = value + decode(pull_in.at[slot], h * (rows_c + CODE_ROWS), rows_c)
        return value

    encode(pulled_rows(1 - zl), pull_z_out, 0)
    p_l = net.start(pull_z_out, pull_z_in, peer_l)

    w_z = {}
    for d in AWAY:
        w_y[d].wait_recv()
    mine_y = weight[pl.ds(x * part_x + y * part_y, part_y), :]
    weight_z[zh] = mine_y + weight_y[0] + weight_y[1] + weight_y[2]
    for d in AWAY:
        w_z[d] = net.start(weight_z.at[zh], weight_z.at[zh], peer_z[d])

    pulled_own = pulled_rows(zl)
    p_l.wait_recv()
    high, low = split_bf16(pulled_own + decode(pull_z_in, 0, rows_c))
    gc_ref[...] = (dot(high, bil_ref[...], NT) + dot(low, bil_ref[...], NT)) * (1.0 / math.sqrt(total_assay))

    g_c[0].wait_recv()
    for d in AWAY:
        g_y[d].wait_recv()

    def grad_rows(h):
        rows = pl.ds(h * rows_a, rows_a)
        value = grads[c, y, rows, :] + grads_in[y, rows, :]
        for slot in range(3):
            value = value + decode(grad_in.at[slot], h * (rows_a + CODE_ROWS), rows_a)
        return value

    g_z = {}
    for d in (2, 1, 3):
        slot = AWAY.index(d)
        encode(grad_rows(turn(zh, d)), grad_z_out.at[slot], 0)
        g_z[d] = net.start(grad_z_out.at[slot], grad_z_in.at[slot], peer_z[d])

    for d in AWAY:
        w_z[d].wait_recv()
    weight_l[0] = (weight_z[0] + weight_z[1]) + (weight_z[2] + weight_z[3])
    w_l = net.start(weight_l.at[0], weight_l.at[1], peer_l)
    grad_own = grad_rows(zh)
    w_l.wait_recv()
    weight_c[0] = weight_l[0] + weight_l[1]
    w_c = net.start(weight_c.at[0], weight_c.at[1], peer_c)
    w_c.wait_recv()
    weight_g[pl.ds(y * part_y, part_y), :] = (weight_c[0] + weight_c[1]) * (
        1.0 / math.sqrt(total_comp * total_assay)
    )
    block = weight_g.at[pl.ds(y * part_y, part_y)]
    w_gy = [net.start(block, block, peer_y[d]) for d in AWAY]
    for copy in w_gy:
        copy.wait_recv()
    gb_ref[pl.ds(x * part_x, part_x), :] = weight_g[...]
    block = gb_ref.at[pl.ds(x * part_x, part_x)]
    w_gx = [net.start(weight_g, block, peer_x[d]) for d in AWAY]

    for d in AWAY:
        g_z[d].wait_recv()
    for slot in range(3):
        grad_own = grad_own + decode(grad_z_in.at[slot], 0, rows_a)
    ga_ref[...] = grad_own * (1.0 / math.sqrt(total_comp))
    for copy in w_gx:
        copy.wait_recv()
    net.finish()


def local(comp_emb, assay_emb, bilinear, tile_pos):
    size_cmp, size_asy = lax.axis_size("cmp"), lax.axis_size("asy")
    rows_c, width = comp_emb.shape
    rows_a = assay_emb.shape[0]
    total_comp, total_assay = rows_c * size_cmp * size_asy, rows_a * size_cmp * size_asy
    group_c, group_a = rows_c * 2, rows_a * RING
    part = width // RING
    vmem = pl.BlockSpec(memory_space=pltpu.VMEM)
    block_c, block_a = rows_c + CODE_ROWS, rows_a + CODE_ROWS
    return tuple(
        pl.pallas_call(
            functools.partial(kernel, (total_comp, total_assay, width)),
            out_shape=[
                jax.ShapeDtypeStruct((rows_c, width), jnp.float32),
                jax.ShapeDtypeStruct((rows_a, width), jnp.float32),
                jax.ShapeDtypeStruct((width, width), jnp.float32),
            ],
            in_specs=[
                pl.BlockSpec(memory_space=pltpu.SMEM),
                pl.BlockSpec(memory_space=pl.ANY),
                pl.BlockSpec(memory_space=pl.ANY),
                vmem,
            ],
            out_specs=[vmem, vmem, vmem],
            scratch_shapes=[
                pltpu.VMEM((RING, group_c, width), jnp.bfloat16),
                pltpu.VMEM((2, RING, group_a, width), jnp.bfloat16),
                pltpu.VMEM((RING, group_c, width), jnp.bfloat16),
                pltpu.VMEM((RING, 2 * RING, group_c, group_a), jnp.bfloat16),
                pltpu.VMEM((RING, group_c, width), jnp.float32),
                pltpu.VMEM((2, RING, group_a, width), jnp.float32),
                pltpu.VMEM((RING, group_a, width), jnp.float32),
                pltpu.VMEM((3, 2 * block_c, width), jnp.int16),
                pltpu.VMEM((3, 2 * block_c, width), jnp.int16),
                pltpu.VMEM((block_c, width), jnp.int16),
                pltpu.VMEM((block_c, width), jnp.int16),
                pltpu.VMEM((3, RING * block_a, width), jnp.int16),
                pltpu.VMEM((3, RING * block_a, width), jnp.int16),
                pltpu.VMEM((3, block_a, width), jnp.int16),
                pltpu.VMEM((3, block_a, width), jnp.int16),
                pltpu.VMEM((width, width), jnp.float32),
                pltpu.VMEM((3, part, width), jnp.float32),
                pltpu.VMEM((3, part // RING, width), jnp.float32),
                pltpu.VMEM((RING, part // RING, width), jnp.float32),
                pltpu.VMEM((2, part // RING, width), jnp.float32),
                pltpu.VMEM((2, part // RING, width), jnp.float32),
                pltpu.VMEM((part, width), jnp.float32),
                pltpu.SemaphoreType.DMA((SENDS,)),
                pltpu.SemaphoreType.DMA((SENDS,)),
                pltpu.SemaphoreType.DMA((2,)),
            ],
            compiler_params=pltpu.CompilerParams(
                collective_id=0, has_side_effects=True, vmem_limit_bytes=58 * 2**20
            ),
            name="link_grads",
        )(tile_pos, comp_emb, assay_emb, bilinear)
    )


def solution(mesh):
    return jax.shard_map(
        local,
        mesh=mesh,
        in_specs=(P(("cmp", "asy"), None), P(("asy", "cmp"), None), P(), P("cmp", "asy")),
        out_specs=(P(("cmp", "asy"), None), P(("asy", "cmp"), None), P()),
        check_vma=False,
    )
```

time: 757 us -> 88.2 us (0.12)
  waiting for transfers between devices: 677 us -> 0 us
  Pallas kernels: 0 us -> 84.3 us
  matrix products: 59.9 us -> 0 us
  between operations: 13.8 us -> 0.66 us
    psum x2 -> x0, waiting for transfers between devices: 536 us -> none  [the longest x1 302 us: local(): whole = lax.psum(grads, 'cmp')]
    all_gather x2 -> x0, waiting for transfers between devices: 85.3 us -> none  [the longest x1 55 us: local(): piece = lax.all_gather(assay_emb, 'cmp', axis=0, tiled=True)]
    pallas_call x0 -> x1, Pallas kernels: none -> 84.3 us  [local(): pl.pallas_call(functools.partial(kernel, (total_comp, total_assay, width)...]
    dot_general x7 -> x0, matrix products: 59.9 us -> none  [the longest x1 20.1 us: local(): lax.dot_general(query, piece, (((1,), (1,)), ((), ())), preferred_element...]
    reduce_scatter x1 -> x0, waiting for transfers between devices: 54.7 us -> none  [local(): lax.psum_scatter(comp_part, 'asy', scatter_dimension=0, tiled=True)]
  transfers between devices with their start and end apart: 5 -> 0, of which waited for: 5 -> 0; matrix products, arithmetic and copies ran while one was open for 4% -> 0% of each run, Pallas kernels for 0% -> 0%
where the time goes in v1:
time: 88.2 us; the launch traced here: 88.1 us
  Pallas kernels  84.3 us (96%)
  local copies, waits for them, and re-layouts  3.09 us (4%)
    pallas_call x1, Pallas kernels, local(): pl.pallas_call(functools.partial(kernel, (total_comp, total_assay, width)...  84.3 us
    unnamed x7, local copies, waits for them, and re-layouts  3.09 us

profile of v1, /device:TPU:32, one launch (start us, length us, event | category | flops | bytes accessed | tf_op | source)
XLA Modules:
  0.0 88.1 jit_solution(3570538065151296336)
XLA Ops:
  0.6 84.3 %link_grads.1 = (f32[256,256]{1,0:T(8,128)}, f32[128,256]{1,0:T(8,128)}, f32[256,256]{1,0:T(8,128)}) custom-call(s32[4,8]{1,0:T(4,128)} %tile_pos.1, bf16[256,256]{1,0:T(8,128)(2,1)} %comp_ref.1, bf16[128,256]{1,0:T(8,128)(2,1)} %assay_ref.1, bf16[256,256]{1,0:T(8,128)(2,1)} %bil_ref.1), custom_call_target="tpu_custom_call" | custom-call | tf_op jit(solution)/shard_map/link_grads/pallas_call | solution.py:413
  85.0 0.0 copy-start.1
  85.0 0.0 copy-start
  85.0 1.7 %copy.10 = f32[256,256]{1,0:T(8,128)} copy(f32[256,256]{1,0:T(8,128)} %get-tuple-element.6) | data formatting | bytes 524288
  86.7 0.0 copy-done.1
  86.7 0.7 copy.11
  87.4 0.0 copy-done
  87.4 0.7 copy.12
Async XLA Ops:
  85.0 1.7 %copy-start.1 = (f32[128,256]{1,0:T(8,128)S(1)}, f32[128,256]{1,0:T(8,128)}, u32[]{:S(2)}) copy-start(f32[128,256]{1,0:T(8,128)} %get-tuple-element.7) | copy-start | bytes 393220
  85.0 2.4 %copy-start = (f32[256,256]{1,0:T(8,128)S(1)}, f32[256,256]{1,0:T(8,128)}, u32[]{:S(2)}) copy-start(f32[256,256]{1,0:T(8,128)} %get-tuple-element.8) | copy-start | bytes 786436

commit v2 on v1

v2 whole, which is shorter than its diff:
```python
import functools
import math

import jax
import jax.numpy as jnp
from jax import lax
from jax.experimental import pallas as pl
from jax.experimental.pallas import tpu as pltpu
from jax.sharding import PartitionSpec as P

MESH = pl.DeviceIdType.MESH
NN = (((1,), (0,)), ((), ()))
NT = (((1,), (1,)), ((), ()))
TN = (((0,), (0,)), ((), ()))
LEVELS = 32000.0
CODE_ROWS = 16
RING = 4
AWAY = (1, 3, 2)
NEAR = (1, 3)


def dot(lhs, rhs, dims):
    return lax.dot_general(lhs, rhs, dims, preferred_element_type=jnp.float32)


def split_bf16(value):
    high = value.astype(jnp.bfloat16)
    low = (value - high.astype(jnp.float32)).astype(jnp.bfloat16)
    return high, low


def encode(value, target, row):
    rows = value.shape[0]
    top = jnp.maximum(jnp.max(jnp.abs(value), axis=0, keepdims=True), 1e-30)
    code = jnp.ceil(jnp.log2(top) * 256.0) + 1.0
    scale = LEVELS * jnp.exp2(code * (-1.0 / 256.0))
    target[pl.ds(row, rows), :] = jnp.round(value * scale).astype(jnp.int32).astype(jnp.int16)
    target[pl.ds(row + rows, CODE_ROWS), :] = (
        jnp.broadcast_to(code, (CODE_ROWS, value.shape[1])).astype(jnp.int32).astype(jnp.int16)
    )


def decode(source, row, rows):
    code = source[pl.ds(row + rows, CODE_ROWS), :].astype(jnp.int32).astype(jnp.float32)[0:1, :]
    unit = jnp.exp2(code * (1.0 / 256.0)) * (1.0 / LEVELS)
    return source[pl.ds(row, rows), :].astype(jnp.int32).astype(jnp.float32) * unit


class Sends:
    def __init__(self, send_sems, recv_sems):
        self.send_sems, self.recv_sems = send_sems, recv_sems
        self.count = 0
        self.started = []

    def make(self, source, target, device):
        index = self.count
        self.count += 1
        return pltpu.make_async_remote_copy(
            src_ref=source,
            dst_ref=target,
            send_sem=self.send_sems.at[index],
            recv_sem=self.recv_sems.at[index],
            device_id=device,
            device_id_type=MESH,
        )

    def start(self, source, target, device):
        copy = self.make(source, target, device)
        copy.start()
        self.started.append(copy)
        return copy

    def finish(self):
        for copy in self.started:
            copy.wait_send()


SENDS = 80


def kernel(
    totals,
    tile_pos,
    comp_ref,
    assay_ref,
    bil_ref,
    gc_ref,
    ga_ref,
    gb_ref,
    comps,
    assays,
    query,
    slope,
    pulled,
    grads,
    grads_out,
    grads_in,
    pull_out,
    pull_in,
    pull_z_out,
    pull_z_in,
    grad_out,
    grad_in,
    grad_z_out,
    grad_z_in,
    weight,
    weight_x,
    weight_y,
    weight_z,
    weight_l,
    weight_c,
    send_sems,
    recv_sems,
    local_sems,
):
    total_comp, total_assay, width = totals
    cmp, asy = lax.axis_index("cmp"), lax.axis_index("asy")
    c, zh, y = cmp % 2, (cmp // 2) % RING, cmp // (2 * RING)
    zl, x = asy % 2, asy // 2
    oc, ol = 1 - c, 1 - zl

    def at(y_=None, zh_=None, c_=None, x_=None, zl_=None):
        y_ = y if y_ is None else y_
        zh_ = zh if zh_ is None else zh_
        c_ = c if c_ is None else c_
        x_ = x if x_ is None else x_
        zl_ = zl if zl_ is None else zl_
        return ((y_ * RING + zh_) * 2 + c_, x_ * 2 + zl_)

    def turn(place, step):
        return lax.rem(place + step, RING)

    peer_c = at(c_=oc)
    peer_l = at(zl_=ol)
    peer_x = {d: at(x_=turn(x, d)) for d in AWAY}
    peer_y = {d: at(y_=turn(y, d)) for d in AWAY}
    peer_z = {d: at(zh_=turn(zh, d)) for d in AWAY}
    partners = [*peer_z.values(), *peer_x.values(), *peer_y.values(), peer_l, peer_c]

    rows_c, rows_a = comp_ref.shape[0], assay_ref.shape[0]
    half_c = RING * rows_c

    def x_rows(x_, count=1):
        return pl.ds(pl.multiple_of(x_ * rows_c, rows_c), count * rows_c)

    def comp_rows(h, x_):
        return comps.at[h, x_rows(x_)]

    def assay_rows(zh_, y_):
        return assays.at[zh_, c, pl.ds(y_ * rows_a, rows_a)]

    def make_query(h, x_):
        block = comps[h, x_rows(x_), :]
        query[h, x_rows(x_), :] = dot(block, bil_ref[...], NN).astype(jnp.bfloat16)

    barrier = pltpu.get_barrier_semaphore()
    for partner in partners:
        pl.semaphore_signal(barrier, inc=1, device_id=partner, device_id_type=MESH)
    own_comp = pltpu.make_async_copy(comp_ref, comp_rows(zl, x), local_sems.at[0])
    own_assay = pltpu.make_async_copy(assay_ref, assay_rows(zh, y), local_sems.at[1])
    own_comp.start()
    own_assay.start()
    own_comp.wait()
    own_assay.wait()
    make_query(zl, x)
    pl.semaphore_wait(barrier, len(partners))

    net = Sends(send_sems, recv_sems)

    a_z, c_x, c_f, a_y, a_f, a_c = {}, {}, {}, {}, {}, {}
    c_l = net.start(comp_ref, comp_rows(zl, x), peer_l)
    for d in NEAR:
        a_z[d] = net.start(assay_ref, assay_rows(zh, y), peer_z[d])
    for d in AWAY:
        a_y[d] = net.start(assay_ref, assay_rows(zh, y), peer_y[d])
        c_x[d] = net.start(comp_ref, comp_rows(zl, x), peer_x[d])

    def share(d):
        block = assays.at[turn(zh, RING - d), c]
        a_c[d] = net.start(block, block, peer_c)

    def spread(d):
        a_z[d].wait_recv()
        block = assay_rows(turn(zh, RING - d), y)
        for e in AWAY:
            a_f[d, e] = net.start(block, block, peer_y[e])

    def gathered(d):
        for e in AWAY:
            a_f[d, e].wait_recv()
        share(d)

    scale = 1.0 / math.sqrt(width)

    def score(h, x_, count, s, first=False):
        rows = x_rows(x_, count)
        q = query[h, rows, :] * jnp.bfloat16(scale)
        total = None
        for cc in range(2):
            chunk = assays[s, cc]
            scores = dot(q, chunk, NT)
            sig = 1.0 / (1.0 + jnp.exp(-scores))
            high = []
            for i in range(count):
                wide = []
                for j in range(RING):
                    label = tile_pos[x_ + i, 2 * j + s // 2].astype(jnp.float32)
                    piece = sig[i * rows_c : (i + 1) * rows_c, j * rows_a : (j + 1) * rows_a]
                    wide.append((piece - label).astype(jnp.bfloat16))
                high.append(jnp.concatenate(wide, axis=1))
            part = high[0] if count == 1 else jnp.concatenate(high, axis=0)
            start = pl.multiple_of(h * half_c + x_ * rows_c, rows_c)
            slope[s, cc, pl.ds(start, count * rows_c), :] = part
            term = dot(part, chunk, NN)
            total = term if total is None else total + term
        pulled[h, rows, :] = total if first else pulled[h, rows, :] + total

    def score_all(h, s, first=False):
        for x_ in (0, 2):
            score(h, x_, 2, s, first)

    s0, s1, s3, s2 = zh, turn(zh, 3), turn(zh, 1), turn(zh, 2)
    c_l.wait_recv()
    block = comp_rows(ol, x)
    for d in NEAR:
        c_f[d] = net.start(block, block, peer_x[d])
    spread(1)
    spread(3)
    a_z[2] = net.start(assay_ref, assay_rows(zh, y), peer_z[2])
    for d in AWAY:
        a_y[d].wait_recv()
    share(0)
    c_f[2] = net.start(block, block, peer_x[2])
    make_query(ol, x)
    for d in AWAY:
        c_x[d].wait_recv()
        make_query(zl, turn(x, RING - d))
    a_c[0].wait_recv()
    score_all(zl, s0, True)
    for d in NEAR:
        c_f[d].wait_recv()
        make_query(ol, turn(x, RING - d))
    for d in (0, 1, 3):
        score(ol, turn(x, d), 1, s0, True)
    spread(2)
    gathered(1)
    c_f[2].wait_recv()
    make_query(ol, turn(x, 2))
    score(ol, turn(x, 2), 1, s0, True)
    a_c[1].wait_recv()
    score_all(zl, s1)
    gathered(3)
    score_all(ol, s1)
    a_c[3].wait_recv()
    score_all(zl, s3)
    gathered(2)
    score_all(ol, s3)
    a_c[2].wait_recv()

    p_x = {}

    def send_pulled(i, h):
        for d in (2, 1, 3):
            slot = AWAY.index(d)
            encode(pulled[h, x_rows(turn(x, d)), :], pull_out.at[slot, i], 0)
            p_x[d, i] = net.start(pull_out.at[slot, i], pull_in.at[slot, i], peer_x[d])

    for i, h in enumerate((ol, zl)):
        score_all(h, s2)
        high, low = split_bf16(pulled[h])
        term = dot(comps[h], high, TN) + dot(comps[h], low, TN)
        if i == 0:
            weight[...] = term
            send_pulled(i, h)
        else:
            weight[...] += term

    part_c = width // 2
    part_x = part_c // RING
    part_y = part_x // RING
    w_x, w_y, w_z = {}, {}, {}
    row_c = c * part_c
    row_x = row_c + x * part_x
    row_y = row_x + y * part_y
    w_c = net.start(weight.at[pl.ds(oc * part_c, part_c)], weight_c, peer_c)

    def weight_at_x():
        w_c.wait_recv()
        mine = weight.at[pl.ds(row_c, part_c)]
        mine[...] += weight_c[...]
        for d in AWAY:
            rows = pl.ds(row_c + turn(x, d) * part_x, part_x)
            w_x[d] = net.start(weight.at[rows], weight_x.at[AWAY.index(d)], peer_x[d])

    g_c, g_y, g_z = {}, {}, {}

    def grad(d, own):
        s = turn(zh, d)
        right = query[...].reshape(2 * half_c, width)
        if own:
            grads[s] = dot(slope[s, c], right, TN)
        else:
            grads_out[s] = dot(slope[s, oc], right, TN)
            g_c[d] = net.start(grads_out.at[s], grads_in.at[s], peer_c)

    def send_grad(d):
        s = turn(zh, d)
        g_c[d].wait_recv()
        for e in AWAY:
            slot = AWAY.index(e)
            rows = pl.ds(turn(y, e) * rows_a, rows_a)
            encode(grads[s, rows, :] + grads_in[s, rows, :], grad_out.at[s, slot], 0)
            g_y[d, e] = net.start(grad_out.at[s, slot], grad_in.at[s, slot], peer_y[e])

    def grad_rows(d):
        s = turn(zh, d)
        rows = pl.ds(y * rows_a, rows_a)
        value = grads[s, rows, :] + grads_in[s, rows, :]
        for e in AWAY:
            g_y[d, e].wait_recv()
        for slot in range(3):
            value = value + decode(grad_in.at[s, slot], 0, rows_a)
        return value

    def forward_grad(d):
        slot = AWAY.index(d)
        encode(grad_rows(d), grad_z_out.at[slot], 0)
        g_z[d] = net.start(grad_z_out.at[slot], grad_z_in.at[slot], peer_z[d])

    def pulled_rows(i, h):
        value = pulled[h, x_rows(x), :]
        for d in AWAY:
            p_x[d, i].wait_recv()
        for slot in range(3):
            value = value + decode(pull_in.at[slot, i], 0, rows_c)
        return value

    def weight_at_y():
        for d in AWAY:
            w_x[d].wait_recv()
        mine = weight.at[pl.ds(row_x, part_x)]
        mine[...] = mine[...] + weight_x[0] + weight_x[1] + weight_x[2]
        for d in AWAY:
            rows = pl.ds(row_x + turn(y, d) * part_y, part_y)
            w_y[d] = net.start(weight.at[rows], weight_y.at[AWAY.index(d)], peer_y[d])

    def weight_at_z():
        for d in AWAY:
            w_y[d].wait_recv()
        weight_z[zh] = weight[pl.ds(row_y, part_y), :] + weight_y[0] + weight_y[1] + weight_y[2]
        for d in AWAY:
            w_z[d] = net.start(weight_z.at[zh], weight_z.at[zh], peer_z[d])

    def weight_at_l():
        for d in AWAY:
            w_z[d].wait_recv()
        weight_l[zl] = (weight_z[0] + weight_z[1]) + (weight_z[2] + weight_z[3])
        return net.start(weight_l.at[zl], weight_l.at[zl], peer_l)

    def weight_back(copies, total):
        for copy in copies:
            copy.wait_recv()
        if total:
            gb_ref[pl.ds(row_y, part_y), :] = (weight_l[0] + weight_l[1]) * (
                1.0 / math.sqrt(total_comp * total_assay)
            )

    def spread_back(row, part, devices):
        block = gb_ref.at[pl.ds(row, part)]
        return [net.start(block, block, device) for device in devices]

    grad(2, False)
    weight_at_x()
    grad(2, True)
    grad(1, False)
    send_grad(2)
    weight_at_y()
    send_pulled(1, zl)
    grad(1, True)
    weight_at_z()
    grad(3, False)
    send_grad(1)
    grad(3, True)
    w_l = weight_at_l()
    grad(0, False)
    send_grad(3)
    weight_back([w_l], True)
    w_gy = spread_back(row_y, part_y, [peer_y[d] for d in AWAY])
    grad(0, True)
    send_grad(0)
    weight_back(w_gy, False)
    w_gx = spread_back(row_x, part_x, [peer_x[d] for d in AWAY])
    encode(pulled_rows(0, ol), pull_z_out, 0)
    p_l = net.start(pull_z_out, pull_z_in, peer_l)
    forward_grad(2)
    weight_back(w_gx, False)
    w_gc = spread_back(row_c, part_c, [peer_c])
    forward_grad(1)
    forward_grad(3)
    pulled_own = pulled_rows(1, zl)
    p_l.wait_recv()
    high, low = split_bf16(pulled_own + decode(pull_z_in, 0, rows_c))
    gc_ref[...] = (dot(high, bil_ref[...], NT) + dot(low, bil_ref[...], NT)) * (1.0 / math.sqrt(total_assay))
    grad_own = grad_rows(0)
    for d in AWAY:
        g_z[d].wait_recv()
    for slot in range(3):
        grad_own = grad_own + decode(grad_z_in.at[slot], 0, rows_a)
    ga_ref[...] = grad_own * (1.0 / math.sqrt(total_comp))
    weight_back(w_gc, False)
    net.finish()


def local(comp_emb, assay_emb, bilinear, tile_pos):
    size_cmp, size_asy = lax.axis_size("cmp"), lax.axis_size("asy")
    rows_c, width = comp_emb.shape
    rows_a = assay_emb.shape[0]
    total_comp, total_assay = rows_c * size_cmp * size_asy, rows_a * size_cmp * size_asy
    half_c, group_a = rows_c * RING, rows_a * RING
    part = width // 2 // RING
    vmem = pl.BlockSpec(memory_space=pltpu.VMEM)
    block_c, block_a = rows_c + CODE_ROWS, rows_a + CODE_ROWS
    return tuple(
        pl.pallas_call(
            functools.partial(kernel, (total_comp, total_assay, width)),
            out_shape=[
                jax.ShapeDtypeStruct((rows_c, width), jnp.float32),
                jax.ShapeDtypeStruct((rows_a, width), jnp.float32),
                jax.ShapeDtypeStruct((width, width), jnp.float32),
            ],
            in_specs=[
                pl.BlockSpec(memory_space=pltpu.SMEM),
                pl.BlockSpec(memory_space=pl.ANY),
                pl.BlockSpec(memory_space=pl.ANY),
                vmem,
            ],
            out_specs=[vmem, vmem, vmem],
            scratch_shapes=[
                pltpu.VMEM((2, half_c, width), jnp.bfloat16),
                pltpu.VMEM((RING, 2, group_a, width), jnp.bfloat16),
                pltpu.VMEM((2, half_c, width), jnp.bfloat16),
                pltpu.VMEM((RING, 2, 2 * half_c, group_a), jnp.bfloat16),
                pltpu.VMEM((2, half_c, width), jnp.float32),
                pltpu.VMEM((RING, group_a, width), jnp.float32),
                pltpu.VMEM((RING, group_a, width), jnp.float32),
                pltpu.VMEM((RING, group_a, width), jnp.float32),
                pltpu.VMEM((3, 2, block_c, width), jnp.int16),
                pltpu.VMEM((3, 2, block_c, width), jnp.int16),
                pltpu.VMEM((block_c, width), jnp.int16),
                pltpu.VMEM((block_c, width), jnp.int16),
                pltpu.VMEM((RING, 3, block_a, width), jnp.int16),
                pltpu.VMEM((RING, 3, block_a, width), jnp.int16),
                pltpu.VMEM((3, block_a, width), jnp.int16),
                pltpu.VMEM((3, block_a, width), jnp.int16),
                pltpu.VMEM((width, width), jnp.float32),
                pltpu.VMEM((3, part, width), jnp.float32),
                pltpu.VMEM((3, part // RING, width), jnp.float32),
                pltpu.VMEM((RING, part // RING, width), jnp.float32),
                pltpu.VMEM((2, part // RING, width), jnp.float32),
                pltpu.VMEM((width // 2, width), jnp.float32),
                pltpu.SemaphoreType.DMA((SENDS,)),
                pltpu.SemaphoreType.DMA((SENDS,)),
                pltpu.SemaphoreType.DMA((2,)),
            ],
            compiler_params=pltpu.CompilerParams(
                collective_id=0, has_side_effects=True, vmem_limit_bytes=58 * 2**20
            ),
            name="link_grads",
        )(tile_pos, comp_emb, assay_emb, bilinear)
    )


def solution(mesh):
    return jax.shard_map(
        local,
        mesh=mesh,
        in_specs=(P(("cmp", "asy"), None), P(("asy", "cmp"), None), P(), P("cmp", "asy")),
        out_specs=(P(("cmp", "asy"), None), P(("asy", "cmp"), None), P()),
        check_vma=False,
    )
```

time: 88.2 us -> 75.7 us (0.86)
  Pallas kernels: 84.3 us -> 71.9 us
    pallas_call x1, Pallas kernels: 84.3 us -> 71.9 us  [local(): pl.pallas_call(functools.partial(kernel, (total_comp, total_assay, width)...]
where the time goes in v2:
time: 75.7 us; the launch traced here: 75.6 us
  Pallas kernels  71.9 us (95%)
  local copies, waits for them, and re-layouts  3.09 us (4%)
    pallas_call x1, Pallas kernels, local(): pl.pallas_call(functools.partial(kernel, (total_comp, total_assay, width)...  71.9 us
    unnamed x7, local copies, waits for them, and re-layouts  3.09 us

profile of v2, /device:TPU:32, one launch (start us, length us, event | category | flops | bytes accessed | tf_op | source)
XLA Modules:
  0.0 75.6 jit_solution(10039259993562979573)
XLA Ops:
  0.6 71.9 %link_grads.1 = (f32[256,256]{1,0:T(8,128)}, f32[128,256]{1,0:T(8,128)}, f32[256,256]{1,0:T(8,128)}) custom-call(s32[4,8]{1,0:T(4,128)} %tile_pos.1, bf16[256,256]{1,0:T(8,128)(2,1)} %comp_ref.1, bf16[128,256]{1,0:T(8,128)(2,1)} %assay_ref.1, bf16[256,256]{1,0:T(8,128)(2,1)} %bil_ref.1), custom_call_target="tpu_custom_call" | custom-call | tf_op jit(solution)/shard_map/link_grads/pallas_call | solution.py:424
  72.5 0.0 copy-start.1
  72.5 0.0 copy-start
  72.5 1.7 %copy.10 = f32[256,256]{1,0:T(8,128)} copy(f32[256,256]{1,0:T(8,128)} %get-tuple-element.6) | data formatting | bytes 524288
  74.2 0.0 copy-done.1
  74.2 0.7 copy.11
  74.9 0.0 copy-done
  74.9 0.7 copy.12
Async XLA Ops:
  72.5 1.7 %copy-start.1 = (f32[128,256]{1,0:T(8,128)S(1)}, f32[128,256]{1,0:T(8,128)}, u32[]{:S(2)}) copy-start(f32[128,256]{1,0:T(8,128)} %get-tuple-element.7) | copy-start | bytes 393220
  72.5 2.4 %copy-start = (f32[256,256]{1,0:T(8,128)S(1)}, f32[256,256]{1,0:T(8,128)}, u32[]{:S(2)}) copy-start(f32[256,256]{1,0:T(8,128)} %get-tuple-element.8) | copy-start | bytes 786436

commit v3 on v2

--- a/solution.py
+++ b/solution.py
@@ -113,7 +113,7 @@
     recv_sems,
     local_sems,
 ):
-    total_comp, total_assay, width = totals
+    width = totals[2]
     cmp, asy = lax.axis_index("cmp"), lax.axis_index("asy")
     c, zh, y = cmp % 2, (cmp // 2) % RING, cmp // (2 * RING)
     zl, x = asy % 2, asy // 2
@@ -218,6 +218,41 @@
     def score_all(h, s, first=False):
         for x_ in (0, 2):
             score(h, x_, 2, s, first)
+
+    g_c, g_y, g_z = {}, {}, {}
+
+    def grad(d, own):
+        s = turn(zh, d)
+        right = query[...].reshape(2 * half_c, width)
+        if own:
+            grads[s] = dot(slope[s, c], right, TN)
+        else:
+            grads_out[s] = dot(slope[s, oc], right, TN)
+            g_c[d] = net.start(grads_out.at[s], grads_in.at[s], peer_c)
+
+    def send_grad(d):
+        s = turn(zh, d)
+        g_c[d].wait_recv()
+        for e in AWAY:
+            slot = AWAY.index(e)
+            rows = pl.ds(turn(y, e) * rows_a, rows_a)
+            encode(grads[s, rows, :] + grads_in[s, rows, :], grad_out.at[s, slot], 0)
+            g_y[d, e] = net.start(grad_out.at[s, slot], grad_in.at[s, slot], peer_y[e])
+
+    def grad_rows(d):
+        s = turn(zh, d)
+        rows = pl.ds(y * rows_a, rows_a)
+        value = grads[s, rows, :] + grads_in[s, rows, :]
+        for e in AWAY:
+            g_y[d, e].wait_recv()
+        for slot in range(3):
+            value = value + decode(grad_in.at[s, slot], 0, rows_a)
+        return value
+
+    def forward_grad(d):
+        slot = AWAY.index(d)
+        encode(grad_rows(d), grad_z_out.at[slot], 0)
+        g_z[d] = net.start(grad_z_out.at[slot], grad_z_in.at[slot], peer_z[d])
 
     s0, s1, s3, s2 = zh, turn(zh, 3), turn(zh, 1), turn(zh, 2)
     c_l.wait_recv()
@@ -251,10 +286,15 @@
     score_all(zl, s1)
     gathered(3)
     score_all(ol, s1)
+    grad(3, False)
     a_c[3].wait_recv()
     score_all(zl, s3)
+    grad(3, True)
     gathered(2)
+    send_grad(3)
     score_all(ol, s3)
+    grad(1, False)
+    grad(1, True)
     a_c[2].wait_recv()
 
     p_x = {}
@@ -267,6 +307,8 @@
 
     for i, h in enumerate((ol, zl)):
         score_all(h, s2)
+        if i == 0:
+            send_grad(1)
         high, low = split_bf16(pulled[h])
         term = dot(comps[h], high, TN) + dot(comps[h], low, TN)
         if i == 0:
@@ -292,41 +334,6 @@
             rows = pl.ds(row_c + turn(x, d) * part_x, part_x)
             w_x[d] = net.start(weight.at[rows], weight_x.at[AWAY.index(d)], peer_x[d])
 
-    g_c, g_y, g_z = {}, {}, {}
-
-    def grad(d, own):
-        s = turn(zh, d)
-        right = query[...].reshape(2 * half_c, width)
-        if own:
-            grads[s] = dot(slope[s, c], right, TN)
-        else:
-            grads_out[s] = dot(slope[s, oc], right, TN)
-            g_c[d] = net.start(grads_out.at[s], grads_in.at[s], peer_c)
-
-    def send_grad(d):
-        s = turn(zh, d)
-        g_c[d].wait_recv()
-        for e in AWAY:
-            slot = AWAY.index(e)
-            rows = pl.ds(turn(y, e) * rows_a, rows_a)
-            encode(grads[s, rows, :] + grads_in[s, rows, :], grad_out.at[s, slot], 0)
-            g_y[d, e] = net.start(grad_out.at[s, slot], grad_in.at[s, slot], peer_y[e])
-
-    def grad_rows(d):
-        s = turn(zh, d)
-        rows = pl.ds(y * rows_a, rows_a)
-        value = grads[s, rows, :] + grads_in[s, rows, :]
-        for e in AWAY:
-            g_y[d, e].wait_recv()
-        for slot in range(3):
-            value = value + decode(grad_in.at[s, slot], 0, rows_a)
-        return value
-
-    def forward_grad(d):
-        slot = AWAY.index(d)
-        encode(grad_rows(d), grad_z_out.at[slot], 0)
-        g_z[d] = net.start(grad_z_out.at[slot], grad_z_in.at[slot], peer_z[d])
-
     def pulled_rows(i, h):
         value = pulled[h, x_rows(x), :]
         for d in AWAY:
@@ -361,9 +368,7 @@
         for copy in copies:
             copy.wait_recv()
         if total:
-            gb_ref[pl.ds(row_y, part_y), :] = (weight_l[0] + weight_l[1]) * (
-                1.0 / math.sqrt(total_comp * total_assay)
-            )
+            gb_ref[pl.ds(row_y, part_y), :] = weight_l[0] + weight_l[1]
 
     def spread_back(row, part, devices):
         block = gb_ref.at[pl.ds(row, part)]
@@ -372,43 +377,44 @@
     grad(2, False)
     weight_at_x()
     grad(2, True)
-    grad(1, False)
     send_grad(2)
+    forward_grad(3)
+    grad(0, False)
     weight_at_y()
     send_pulled(1, zl)
-    grad(1, True)
+    grad(0, True)
     weight_at_z()
-    grad(3, False)
-    send_grad(1)
-    grad(3, True)
+    send_grad(0)
+    forward_grad(1)
     w_l = weight_at_l()
-    grad(0, False)
-    send_grad(3)
+    encode(pulled_rows(0, ol), pull_z_out, 0)
+    p_l = net.start(pull_z_out, pull_z_in, peer_l)
     weight_back([w_l], True)
     w_gy = spread_back(row_y, part_y, [peer_y[d] for d in AWAY])
-    grad(0, True)
-    send_grad(0)
+    forward_grad(2)
     weight_back(w_gy, False)
     w_gx = spread_back(row_x, part_x, [peer_x[d] for d in AWAY])
-    encode(pulled_rows(0, ol), pull_z_out, 0)
-    p_l = net.start(pull_z_out, pull_z_in, peer_l)
-    forward_grad(2)
-    weight_back(w_gx, False)
-    w_gc = spread_back(row_c, part_c, [peer_c])
-    forward_grad(1)
-    forward_grad(3)
     pulled_own = pulled_rows(1, zl)
     p_l.wait_recv()
     high, low = split_bf16(pulled_own + decode(pull_z_in, 0, rows_c))
-    gc_ref[...] = (dot(high, bil_ref[...], NT) + dot(low, bil_ref[...], NT)) * (1.0 / math.sqrt(total_assay))
+    gc_ref[...] = dot(high, bil_ref[...], NT) + dot(low, bil_ref[...], NT)
+    weight_back(w_gx, False)
+    w_gc = spread_back(row_c, part_c, [peer_c])
     grad_own = grad_rows(0)
     for d in AWAY:
         g_z[d].wait_recv()
     for slot in range(3):
         grad_own = grad_own + decode(grad_z_in.at[slot], 0, rows_a)
-    ga_ref[...] = grad_own * (1.0 / math.sqrt(total_comp))
+    ga_ref[...] = grad_own
     weight_back(w_gc, False)
     net.finish()
+
+
+def scale_kernel(totals, gc_in, ga_in, gb_in, gc_ref, ga_ref, gb_ref):
+    total_comp, total_assay, _ = totals
+    gc_ref[...] = gc_in[...] * (1.0 / math.sqrt(total_assay))
+    ga_ref[...] = ga_in[...] * (1.0 / math.sqrt(total_comp))
+    gb_ref[...] = gb_in[...] * (1.0 / math.sqrt(total_comp * total_assay))
 
 
 def local(comp_emb, assay_emb, bilinear, tile_pos):
@@ -420,14 +426,16 @@
     part = width // 2 // RING
     vmem = pl.BlockSpec(memory_space=pltpu.VMEM)
     block_c, block_a = rows_c + CODE_ROWS, rows_a + CODE_ROWS
-    return tuple(
+    totals = (total_comp, total_assay, width)
+    shapes = [
+        jax.ShapeDtypeStruct((rows_c, width), jnp.float32),
+        jax.ShapeDtypeStruct((rows_a, width), jnp.float32),
+        jax.ShapeDtypeStruct((width, width), jnp.float32),
+    ]
+    sums = (
         pl.pallas_call(
-            functools.partial(kernel, (total_comp, total_assay, width)),
-            out_shape=[
-                jax.ShapeDtypeStruct((rows_c, width), jnp.float32),
-                jax.ShapeDtypeStruct((rows_a, width), jnp.float32),
-                jax.ShapeDtypeStruct((width, width), jnp.float32),
-            ],
+            functools.partial(kernel, totals),
+            out_shape=shapes,
             in_specs=[
                 pl.BlockSpec(memory_space=pltpu.SMEM),
                 pl.BlockSpec(memory_space=pl.ANY),
@@ -468,6 +476,15 @@
             name="link_grads",
         )(tile_pos, comp_emb, assay_emb, bilinear)
     )
+    return tuple(
+        pl.pallas_call(
+            functools.partial(scale_kernel, totals),
+            out_shape=shapes,
+            in_specs=[vmem, vmem, vmem],
+            out_specs=[vmem, vmem, vmem],
+            name="scale_grads",
+        )(*sums)
+    )
 
 
 def solution(mesh):

time: 75.7 us -> 74.9 us (0.989); the launches traced: 75.6 us -> 73.6 us
  local copies, waits for them, and re-layouts: 3.09 us -> 0 us
  Pallas kernels: 71.9 us -> 72.9 us
    unnamed x7 -> x0, local copies, waits for them, and re-layouts: 3.09 us -> none
    pallas_call x1 -> x2, Pallas kernels: 71.9 us -> 72.9 us  [the longest x1 71 us: local(): pl.pallas_call(functools.partial(kernel, totals), out_shape=shapes, in_sp...]
where the time goes in v3:
time: 74.9 us; the launch traced here: 73.6 us
  Pallas kernels  72.9 us (97%)
    pallas_call x1, Pallas kernels, local(): pl.pallas_call(functools.partial(kernel, totals), out_shape=shapes, in_sp...  71 us
    pallas_call x1, Pallas kernels, local(): pl.pallas_call(functools.partial(scale_kernel, totals), out_shape=shapes,...  1.95 us

profile of v3, /device:TPU:32, one launch (start us, length us, event | category | flops | bytes accessed | tf_op | source)
XLA Modules:
  0.0 73.6 jit_solution(9975907396740908849)
XLA Ops:
  0.6 71.0 %link_grads.1 = (f32[256,256]{1,0:T(8,128)}, f32[128,256]{1,0:T(8,128)}, f32[256,256]{1,0:T(8,128)}) custom-call(s32[4,8]{1,0:T(4,128)} %tile_pos.1, bf16[256,256]{1,0:T(8,128)(2,1)} %comp_ref.1, bf16[128,256]{1,0:T(8,128)(2,1)} %assay_ref.1, bf16[256,256]{1,0:T(8,128)(2,1)} %bil_ref.1), custom_call_target="tpu_custom_call" | custom-call | tf_op jit(solution)/shard_map/link_grads/pallas_call | solution.py:436
  71.6 1.9 %scale_grads.1 = (f32[256,256]{1,0:T(8,128)}, f32[128,256]{1,0:T(8,128)}, f32[256,256]{1,0:T(8,128)}) custom-call(f32[256,256]{1,0:T(8,128)} %get-tuple-element.6.gc_in, f32[128,256]{1,0:T(8,128)} %get-tuple-element.7.ga_in, f32[256,256]{1,0:T(8,128)} %get-tuple-element.8.gb_in), custom_call_target="tpu_custom_call" | custom-call | tf_op jit(solution)/shard_map/scale_grads/pallas_call | solution.py:480

commit v4 on v3

--- a/solution.py
+++ b/solution.py
@@ -376,12 +376,12 @@
 
     grad(2, False)
     weight_at_x()
+    send_pulled(1, zl)
     grad(2, True)
     send_grad(2)
     forward_grad(3)
     grad(0, False)
     weight_at_y()
-    send_pulled(1, zl)
     grad(0, True)
     weight_at_z()
     send_grad(0)

time: 74.9 us -> 75 us (level)
  no operation moved by 1% of the time
where the time goes in v4:
time: 75 us; the launch traced here: 73.6 us
  Pallas kernels  73 us (97%)
    pallas_call x1, Pallas kernels, local(): pl.pallas_call(functools.partial(kernel, totals), out_shape=shapes, in_sp...  71 us
    pallas_call x1, Pallas kernels, local(): pl.pallas_call(functools.partial(scale_kernel, totals), out_shape=shapes,...  1.95 us

profile of v4, /device:TPU:32, one launch (start us, length us, event | category | flops | bytes accessed | tf_op | source)
XLA Modules:
  0.0 73.6 jit_solution(11483363253939272121)
XLA Ops:
  0.6 71.0 %link_grads.1 = (f32[256,256]{1,0:T(8,128)}, f32[128,256]{1,0:T(8,128)}, f32[256,256]{1,0:T(8,128)}) custom-call(s32[4,8]{1,0:T(4,128)} %tile_pos.1, bf16[256,256]{1,0:T(8,128)(2,1)} %comp_ref.1, bf16[128,256]{1,0:T(8,128)(2,1)} %assay_ref.1, bf16[256,256]{1,0:T(8,128)(2,1)} %bil_ref.1), custom_call_target="tpu_custom_call" | custom-call | tf_op jit(solution)/shard_map/link_grads/pallas_call | solution.py:436
  71.6 1.9 %scale_grads.1 = (f32[256,256]{1,0:T(8,128)}, f32[128,256]{1,0:T(8,128)}, f32[256,256]{1,0:T(8,128)}) custom-call(f32[256,256]{1,0:T(8,128)} %get-tuple-element.6.gc_in, f32[128,256]{1,0:T(8,128)} %get-tuple-element.7.ga_in, f32[256,256]{1,0:T(8,128)} %get-tuple-element.8.gb_in), custom_call_target="tpu_custom_call" | custom-call | tf_op jit(solution)/shard_map/scale_grads/pallas_call | solution.py:480
